TPU v7x, 512 devices: a whole 4x4x16 slice. The times are simulated.
512 devices in a mesh: stream: 4 (over x), span: 8 (over y, core), normal: 16 (over z).
Axes of the slice: x: 4, y: 4, z: 16, core: 2. Of those that a mesh axis runs over, the one named last changes fastest.
Arguments:
- state: float32 [5, 512, 64, 512], P(None, 'normal', 'span', 'stream'), may hold values from -5 to 5
- speeds: float32 [3, 512, 64, 512], P(None, 'normal', 'span', 'stream'), may hold values from -4 to 4
- damping: float32 [512, 64, 512], P('normal', 'span', 'stream'), may hold values from 0.02 to 0.2
- source: float32 [5, 512, 64, 512], P(None, 'normal', 'span', 'stream'), may hold values from -5 to 5.5
- normal_stiff: float32 [512, 64, 512], P('normal', 'span', 'stream'), may hold values from 10 to 1000
- wide_stiff: float32 [512, 64, 512], P('normal', 'span', 'stream'), may hold values from 2 to 200
- char_rates: float32 [5], replicated, may hold values from 0.5 to 2
- left_vectors: float32 [5, 5], replicated, may hold values from -0.6 to 2.1
- right_vectors: float32 [5, 5], replicated, may hold values from -0.6 to 2.1
Outputs:
- update: float32 [5, 512, 64, 512], P(None, 'normal', 'span', 'stream')
All inputs are finite; a program needn't handle non-finite values.
Results may differ from a plain program's by a relative error of at most 0.0003.
Values sent between devices are 32-bit elements; how exact they have to be, the bound alone decides.
A program may use at most 128 MiB of HBM per device.

v0:
```python
import functools

import jax
import jax.numpy as jnp
from jax import lax
from jax.experimental import pallas as pl
from jax.experimental.pallas import tpu as pltpu
from jax.sharding import PartitionSpec as P

MESH = pl.DeviceIdType.MESH
NV = 5
F32 = jnp.float32


def kernel(
    nstream, nspan, nnorm,
    state, speeds, damping, source, nstiff, wstiff, rates, left, right,
    out,
    st, spz, spy, spx, dmp, src, ns, ws,
    yh, xpack, xh_l, xh_r,
    inv_s, m_s, far_s, near_s, a_s, b_s, v_s,
    ab_send, ab_recv, de, pq, rc,
    w_send, w_recv, vrow, rr_send, rr, tri, sp, xsep, o_s, consts,
    load_sem, out_sem, halo_send, halo_recv, nb_send, nb_recv,
    c_send, c_recv, r_send, r_recv, s_send, s_recv,
):
    K = nstiff.shape[0]
    sx = lax.axis_index("stream")
    sy = lax.axis_index("span")
    sz = lax.axis_index("normal")
    x_next, x_prev = lax.rem(sx + 1, nstream), lax.rem(sx + nstream - 1, nstream)
    y_next, y_prev = lax.rem(sy + 1, nspan), lax.rem(sy + nspan - 1, nspan)
    z_next, z_prev = lax.rem(sz + 1, nnorm), lax.rem(sz + nnorm - 1, nnorm)
    at_xn, at_xp = (x_next, sy, sz), (x_prev, sy, sz)
    at_yn, at_yp = (sx, y_next, sz), (sx, y_prev, sz)
    at_zn, at_zp = (sx, sy, z_next), (sx, sy, z_prev)

    loads = [
        (nstiff, ns), (wstiff, ws), (state, st.at[:, 2:K + 2]), (speeds.at[2], spx), (speeds.at[0], spz.at[2:K + 2]),
        (speeds.at[1], spy), (damping, dmp), (source, src),
    ]
    load = [pltpu.make_async_copy(a, b, load_sem.at[i]) for i, (a, b) in enumerate(loads)]
    for c in load:
        c.start()

    barrier = pltpu.get_barrier_semaphore()
    for there in (at_xn, at_xp, at_yn, at_yp):
        pl.semaphore_signal(barrier, inc=1, device_id=there, device_id_type=MESH)

    @pl.loop(1, nnorm)
    def _(d):
        pl.semaphore_signal(barrier, inc=1, device_id=(sx, sy, lax.rem(sz + d, nnorm)), device_id_type=MESH)

    pl.semaphore_wait(barrier, nnorm + 3)

    def remote(a, b, s, r, there):
        return pltpu.make_async_remote_copy(
            src_ref=a, dst_ref=b, send_sem=s, recv_sem=r, device_id=there, device_id_type=MESH
        )

    halo_list = [
        (state.at[:, :, 6:8, :], yh.at[0:NV, :, 6:8, :], at_yn),
        (state.at[:, :, 0:2, :], yh.at[0:NV, :, 0:2, :], at_yp),
        (speeds.at[1, :, 6:8, :], yh.at[NV, :, 6:8, :], at_yn),
        (speeds.at[1, :, 0:2, :], yh.at[NV, :, 0:2, :], at_yp),
        (state.at[:, K - 2:K], st.at[:, 0:2], at_zn),
        (state.at[:, 0:2], st.at[:, K + 2:K + 4], at_zp),
        (speeds.at[0, K - 2:K], spz.at[0:2], at_zn),
        (speeds.at[0, 0:2], spz.at[K + 2:K + 4], at_zp),
    ]
    halos = [
        remote(a, b, halo_send.at[i], halo_recv.at[i], there) for i, (a, b, there) in enumerate(halo_list)
    ]
    for c in halos:
        c.start()

    lane = lax.broadcasted_iota(jnp.int32, (8, 128), 1)
    row = lax.broadcasted_iota(jnp.int32, (8, 128), 0)

    load[2].wait()
    load[3].wait()
    quad = lane // 4

    def pack(k, acc):
        here = quad == k
        tiles = [st[v, k + 2] for v in range(NV)] + [spx[k]]
        return tuple(jnp.where(here, pltpu.roll(t, 4 * k + 2, 1), a) for t, a in zip(tiles, acc))

    packed = lax.fori_loop(0, K, pack, tuple(spx[0] for _ in range(NV + 1)))
    for i, p in enumerate(packed):
        xpack[i] = p
    xcopies = [
        remote(xpack, xh_l, halo_send.at[8], halo_recv.at[8], at_xn),
        remote(xpack, xh_r, halo_send.at[9], halo_recv.at[9], at_xp),
    ]
    for c in xcopies:
        c.start()

    load[0].wait()
    load[1].wait()
    consts[0] = jnp.zeros((8, 128), F32)
    consts[1] = jnp.ones((8, 128), F32)
    zero, one = consts[0], consts[1]

    def factor(k, carry):
        g0, h0 = ns[k], ws[k]
        new = []
        for c in range(NV):
            near_p, far_p, a_p, b_p, near_b, far_b, a_b, b_b = carry[c]
            rate = rates[c]
            g, h = rate * g0, rate * h0
            low = h * near_b - g
            diag = (1.0 + 2.0 * (g + h)) + h * far_b - low * near_p
            inv = 1.0 / diag
            m = low * inv
            hi = h * inv
            near = (-g - low * far_p) * inv
            a = hi * a_b - m * a_p
            b = hi * b_b - m * b_p
            inv_s[c, k] = inv
            m_s[c, k] = m
            far_s[c, k] = hi
            near_s[c, k] = near
            a_s[c, k] = a
            b_s[c, k] = b
            new.append((near, -hi, a, b, near_p, far_p, a_p, b_p))
        return tuple(new)

    lax.fori_loop(0, K, factor, tuple((zero, zero, zero, one, zero, zero, one, zero) for _ in range(NV)))

    def spikes(i, carry):
        k = K - 3 - i
        new = []
        for c in range(NV):
            near, hi = near_s[c, k], far_s[c, k]
            ones = carry[c][0:4]
            twos = carry[c][4:8]
            base = (a_s[c, k], b_s[c, k], None, None)
            fresh = []
            for o, t, q in zip(ones, twos, base):
                r = hi * t - near * o
                fresh.append(r if q is None else r + q)
            new.append(tuple(fresh) + ones)
        return tuple(new)

    start = (zero, zero, one, zero, zero, zero, zero, one)
    done = lax.fori_loop(0, K - 2, spikes, tuple(start for _ in range(NV)))
    for c in range(NV):
        r0, r1 = done[c][0:4], done[c][4:8]
        for e, val in enumerate((r0[0], r0[1], r1[0], r1[1], r0[2], r0[3], r1[2], r1[3])):
            ab_send[e, c] = val
    ab_copy = remote(ab_send, ab_recv, nb_send.at[0], nb_recv.at[0], at_zp)
    ab_copy.start()

    is_last = sz == nnorm - 1
    ab_copy.wait_recv()

    @pl.when(is_last)
    def _():
        @pl.loop(0, 8)
        def _(e):
            for c in range(NV):
                ab_recv[e, c] = zero

    @pl.loop(0, NV)
    def _(c):
        n30, n31, h30, h31 = near_s[c, K - 2], near_s[c, K - 1], far_s[c, K - 2], far_s[c, K - 1]
        a30, a31, b30, b31 = a_s[c, K - 2], a_s[c, K - 1], b_s[c, K - 2], b_s[c, K - 1]
        n00, n01, n10, n11 = n30 * n31 + h30, -n30 * h31, -n31, h31
        s00, s01, s10, s11 = a30 - n30 * a31, b30 - n30 * b31, a31, b31
        A00, A01, A10, A11 = ab_recv[0, c], ab_recv[1, c], ab_recv[2, c], ab_recv[3, c]
        B00, B01, B10, B11 = ab_recv[4, c], ab_recv[5, c], ab_recv[6, c], ab_recv[7, c]
        m00 = 1.0 - (n00 * A00 + n01 * A10)
        m01 = -(n00 * A01 + n01 * A11)
        m10 = -(n10 * A00 + n11 * A10)
        m11 = 1.0 - (n10 * A01 + n11 * A11)
        det = 1.0 / (m00 * m11 - m01 * m10)
        d00, d01, d10, d11 = m11 * det, -m01 * det, -m10 * det, m00 * det
        e00, e01 = d00 * n00 + d01 * n10, d00 * n01 + d01 * n11
        e10, e11 = d10 * n00 + d11 * n10, d10 * n01 + d11 * n11
        for i, val in enumerate((d00, d01, d10, d11, e00, e01, e10, e11)):
            de[i, c] = val
        pq[0, c] = d00 * s00 + d01 * s10
        pq[1, c] = d00 * s01 + d01 * s11
        pq[2, c] = d10 * s00 + d11 * s10
        pq[3, c] = d10 * s01 + d11 * s11
        pq[4, c] = e00 * B00 + e01 * B10
        pq[5, c] = e00 * B01 + e01 * B11
        pq[6, c] = e10 * B00 + e11 * B10
        pq[7, c] = e10 * B01 + e11 * B11

    def scatter(rows, land, s, r, t):
        return remote(
            rows.at[:, pl.ds(2 * (t // 8), 3), lax.rem(t, 8), :], land.at[sz, :, 0:3, :],
            s.at[t], r.at[sz], (sx, sy, t),
        )

    def scatter_in(rows, land, s, r, t):
        return remote(
            rows.at[:, pl.ds(0, 3), 0, :], land.at[t, :, 0:3, :],
            s.at[t], r.at[t], (sx, sy, t),
        )

    def scatter_own(rows, land, r):
        return pltpu.make_async_copy(
            rows.at[:, pl.ds(2 * (sz // 8), 3), lax.rem(sz, 8), :], land.at[sz, :, 0:3, :], r.at[sz]
        )

    def send_all(rows, land, s, r):
        @pl.loop(1, nnorm)
        def _(d):
            scatter(rows, land, s, r, lax.rem(sz + d, nnorm)).start()

        scatter_own(rows, land, r).start()

    def recv_all(rows, land, s, r):
        @pl.loop(1, nnorm)
        def _(d):
            scatter_in(rows, land, s, r, lax.rem(sz + d, nnorm)).wait_recv()

        scatter_own(rows, land, r).wait()

    def drain_all(rows, land, s, r):
        @pl.loop(1, nnorm)
        def _(d):
            scatter(rows, land, s, r, lax.rem(sz + d, nnorm)).wait_send()

    send_all(pq, rc, c_send, c_recv)

    for c in load[4:8]:
        c.wait()
    for c in halos:
        c.wait_recv()
    for c in xcopies:
        c.wait_recv()

    @pl.when(sz == 0)
    def _():
        for v in range(NV):
            st[v, 0] = zero
            st[v, 1] = zero

    @pl.when(is_last)
    def _():
        for v in range(NV):
            st[v, K + 2] = zero
            st[v, K + 3] = zero

    take_left = lax.rem(lane, 4) < 2
    for i in range(NV + 1):
        xpack_h = jnp.where(take_left, xh_l[i], xh_r[i])
        xh_l[i] = xpack_h

    def gate(inside, ok):
        return jnp.where(inside, one, jnp.where(ok, 1.0, 0.0).astype(F32) * one)

    has_xn, has_xp = sx < nstream - 1, sx > 0
    has_yn, has_yp = sy < nspan - 1, sy > 0
    gx_p1, gx_p2 = gate(lane < 127, has_xn), gate(lane < 126, has_xn)
    gx_m1, gx_m2 = gate(lane > 0, has_xp), gate(lane > 1, has_xp)
    gy_p1, gy_p2 = gate(row < 7, has_yn), gate(row < 6, has_yn)
    gy_m1, gy_m2 = gate(row > 0, has_yp), gate(row > 1, has_yp)

    def around(t, h, index, size, axis):
        return (
            pltpu.roll(jnp.where(index < 1, h, t), size - 1, axis),
            pltpu.roll(jnp.where(index < 2, h, t), size - 2, axis),
            pltpu.roll(jnp.where(index >= size - 1, h, t), 1, axis),
            pltpu.roll(jnp.where(index >= size - 2, h, t), 2, axis),
        )

    C1, C2 = 2.0 / 3.0, 1.0 / 12.0

    def level(k, carry):
        d = dmp[k]
        d4 = 4.0 * d
        shift = 126 - 4 * k
        hx = [pltpu.roll(xh_l[i], shift, 1) for i in range(NV + 1)]
        xp1, xp2, xm1, xm2 = around(spx[k], hx[NV], lane, 128, 1)
        yp1, yp2, ym1, ym2 = around(spy[k], yh[NV, k], row, 8, 0)
        zm2, zm1, zp1, zp2 = spz[k], spz[k + 1], spz[k + 3], spz[k + 4]
        wx = ((d4 - C1 * xp1) * gx_p1, (C2 * xp2 - d) * gx_p2, (d4 + C1 * xm1) * gx_m1, (-d - C2 * xm2) * gx_m2)
        wy = ((d4 - C1 * yp1) * gy_p1, (C2 * yp2 - d) * gy_p2, (d4 + C1 * ym1) * gy_m1, (-d - C2 * ym2) * gy_m2)
        wz = (d4 - C1 * zp1, C2 * zp2 - d, d4 + C1 * zm1, -d - C2 * zm2)
        wc = -18.0 * d
        rhs = []
        for v in range(NV):
            t = st[v, k + 2]
            acc = src[v, k] + wc * t
            zs = (st[v, k + 3], st[v, k + 4], st[v, k + 1], st[v, k])
            accz = wz[0] * zs[0] + wz[1] * zs[1] + wz[2] * zs[2] + wz[3] * zs[3]
            xs = around(t, hx[v], lane, 128, 1)
            accx = wx[0] * xs[0] + wx[1] * xs[1] + wx[2] * xs[2] + wx[3] * xs[3]
            ys = around(t, yh[v, k], row, 8, 0)
            accy = wy[0] * ys[0] + wy[1] * ys[1] + wy[2] * ys[2] + wy[3] * ys[3]
            rhs.append((acc + accz) + (accx + accy))
        new = []
        for c in range(NV):
            f = left[c, 0] * rhs[0]
            for v in range(1, NV):
                f = f + left[c, v] * rhs[v]
            one_back, two_back = carry[c]
            val = f * inv_s[c, k] + far_s[c, k] * two_back - m_s[c, k] * one_back
            v_s[c, k] = val
            new.append((val, one_back))
        return tuple(new)

    ends = lax.fori_loop(0, K, level, tuple((zero, zero) for _ in range(NV)))

    def back(i, carry):
        k = K - 3 - i
        return tuple(
            (v_s[c, k] + far_s[c, k] * carry[c][1] - near_s[c, k] * carry[c][0], carry[c][0]) for c in range(NV)
        )

    firsts = lax.fori_loop(0, K - 2, back, tuple((zero, zero) for _ in range(NV)))
    for c in range(NV):
        w_send[0, c] = firsts[c][0]
        w_send[1, c] = firsts[c][1]
        v31, v30 = ends[c]
        vrow[0, c] = v30 - near_s[c, K - 2] * v31
        vrow[1, c] = v31
    w_copy = remote(w_send, w_recv, nb_send.at[1], nb_recv.at[1], at_zp)
    w_copy.start()

    recv_all(pq, rc, c_send, c_recv)

    def block_factor(j, carry):
        t00, t01, t10, t11 = carry
        p00, p01, p10, p11, q00, q01, q10, q11 = [rc[j, e] for e in range(8)]
        m00 = 1.0 - (p00 * t00 + p01 * t10)
        m01 = -(p00 * t01 + p01 * t11)
        m10 = -(p10 * t00 + p11 * t10)
        m11 = 1.0 - (p10 * t01 + p11 * t11)
        det = 1.0 / (m00 * m11 - m01 * m10)
        d00, d01, d10, d11 = m11 * det, -m01 * det, -m10 * det, m00 * det
        t00, t01 = d00 * q00 + d01 * q10, d00 * q01 + d01 * q11
        t10, t11 = d10 * q00 + d11 * q10, d10 * q01 + d11 * q11
        vals = (
            d00, d01, d10, d11,
            d00 * p00 + d01 * p10, d00 * p01 + d01 * p11, d10 * p00 + d11 * p10, d10 * p01 + d11 * p11,
            t00, t01, t10, t11,
        )
        for i, val in enumerate(vals):
            tri[j, i] = val
        return (t00, t01, t10, t11)

    lax.fori_loop(0, nnorm, block_factor, (zero, zero, zero, zero))

    w_copy.wait_recv()

    @pl.when(is_last)
    def _():
        for c in range(NV):
            w_recv[0, c] = zero
            w_recv[1, c] = zero

    for c in range(NV):
        v0, v1, w0, w1 = vrow[0, c], vrow[1, c], w_recv[0, c], w_recv[1, c]
        rr_send[0, c] = (de[0, c] * v0 + de[1, c] * v1) + (de[4, c] * w0 + de[5, c] * w1)
        rr_send[1, c] = (de[2, c] * v0 + de[3, c] * v1) + (de[6, c] * w0 + de[7, c] * w1)
    send_all(rr_send, rr, r_send, r_recv)
    recv_all(rr_send, rr, r_send, r_recv)

    def block_forward(j, carry):
        z0, z1 = carry
        r0, r1 = rr[j, 0], rr[j, 1]
        n0 = (tri[j, 0] * r0 + tri[j, 1] * r1) + (tri[j, 4] * z0 + tri[j, 5] * z1)
        n1 = (tri[j, 2] * r0 + tri[j, 3] * r1) + (tri[j, 6] * z0 + tri[j, 7] * z1)
        rr[j, 0] = n0
        rr[j, 1] = n1
        return (n0, n1)

    lax.fori_loop(0, nnorm, block_forward, (zero, zero))

    def block_back(i, carry):
        j = nnorm - 1 - i
        s0, s1 = carry
        n0 = rr[j, 0] + (tri[j, 8] * s0 + tri[j, 9] * s1)
        n1 = rr[j, 1] + (tri[j, 10] * s0 + tri[j, 11] * s1)
        sp[j + 1, 0] = n0
        sp[j + 1, 1] = n1
        return (n0, n1)

    lax.fori_loop(0, nnorm, block_back, (zero, zero))
    sp[0, 0] = zero
    sp[0, 1] = zero

    def home(t):
        return remote(
            sp.at[pl.ds(t, 2), :, 0:3, :], xsep.at[:, :, pl.ds(3 * (sz // 8), 3), lax.rem(sz, 8), :],
            s_send.at[t], s_recv.at[sz], (sx, sy, t),
        )

    def home_in(t):
        return remote(
            sp.at[pl.ds(0, 2), :, 0:3, :], xsep.at[:, :, pl.ds(3 * (t // 8), 3), lax.rem(t, 8), :],
            s_send.at[t], s_recv.at[t], (sx, sy, t),
        )

    home_own = pltpu.make_async_copy(
        sp.at[pl.ds(sz, 2), :, 0:3, :], xsep.at[:, :, pl.ds(3 * (sz // 8), 3), lax.rem(sz, 8), :], s_recv.at[sz]
    )

    @pl.loop(1, nnorm)
    def _(d):
        home(lax.rem(sz + d, nnorm)).start()

    home_own.start()

    @pl.loop(1, nnorm)
    def _(d):
        home_in(lax.rem(sz + d, nnorm)).wait_recv()

    home_own.wait()

    slot = (0, 1, 2, 4, 5)
    pre = [(xsep[0, 0, slot[c]], xsep[0, 1, slot[c]]) for c in range(NV)]
    own_s = [(xsep[1, 0, slot[c]], xsep[1, 1, slot[c]]) for c in range(NV)]

    def emit(k, xs):
        for v in range(NV):
            u = right[v, 0] * xs[0]
            for c in range(1, NV):
                u = u + right[v, c] * xs[c]
            o_s[v, k] = u

    emit(K - 1, [s[1] for s in own_s])
    emit(K - 2, [s[0] for s in own_s])

    def final(i, carry):
        k = K - 3 - i
        new = []
        for c in range(NV):
            known = v_s[c, k] + (a_s[c, k] * xsep[0, 0, slot[c]] + b_s[c, k] * xsep[0, 1, slot[c]])
            val = known + far_s[c, k] * carry[c][1] - near_s[c, k] * carry[c][0]
            new.append((val, carry[c][0]))
        emit(k, [n[0] for n in new])
        return tuple(new)

    lax.fori_loop(0, K - 2, final, tuple(own_s))
    put = pltpu.make_async_copy(o_s, out, out_sem)
    put.start()

    for c in halos:
        c.wait_send()
    for c in xcopies:
        c.wait_send()
    ab_copy.wait_send()
    w_copy.wait_send()
    drain_all(pq, rc, c_send, c_recv)
    drain_all(rr_send, rr, r_send, r_recv)

    @pl.loop(1, nnorm)
    def _(d):
        home(lax.rem(sz + d, nnorm)).wait_send()

    put.wait()


def solution(mesh):
    nstream, nspan, nnorm = mesh.shape["stream"], mesh.shape["span"], mesh.shape["normal"]

    def step(state, speeds, damping, source, normal_stiff, wide_stiff, char_rates, left_vectors, right_vectors):
        K = damping.shape[0]
        T = damping.shape[1:]
        vm = lambda *s: pltpu.VMEM(s + T, F32)
        dma = lambda n: pltpu.SemaphoreType.DMA((n,))
        hbm = pl.BlockSpec(memory_space=pltpu.HBM)
        smem = pl.BlockSpec(memory_space=pltpu.SMEM)
        per = lambda: vm(NV, K)
        return pl.pallas_call(
            functools.partial(kernel, nstream, nspan, nnorm),
            out_shape=jax.ShapeDtypeStruct(state.shape, F32),
            in_specs=[hbm] * 6 + [smem] * 3,
            out_specs=hbm,
            scratch_shapes=[
                vm(NV, K + 4), vm(K + 4), vm(K), vm(K), vm(K), vm(NV, K), vm(K), vm(K),
                vm(NV + 1, K), vm(NV + 1), vm(NV + 1), vm(NV + 1),
                per(), per(), per(), per(), per(), per(), per(),
                vm(8, NV), vm(8, NV), vm(8, NV), vm(8, NV), vm(nnorm, 8),
                vm(2, NV), vm(2, NV), vm(2, NV), vm(2, NV), vm(nnorm, 2), vm(nnorm, 12), vm(nnorm + 1, 2),
                vm(2, 2, 6), vm(NV, K), vm(2),
                dma(8), pltpu.SemaphoreType.DMA, dma(10), dma(10), dma(2), dma(2),
                dma(nnorm), dma(nnorm), dma(nnorm), dma(nnorm), dma(nnorm), dma(nnorm),
            ],
            compiler_params=pltpu.CompilerParams(
                collective_id=0, has_side_effects=True, vmem_limit_bytes=32 * 1024 * 1024
            ),
            cost_estimate=pl.CostEstimate(flops=20_000_000, bytes_accessed=2_900_000, transcendentals=0),
        )(state, speeds, damping, source, normal_stiff, wide_stiff, char_rates, left_vectors, right_vectors)

    fields = P(None, "normal", "span", "stream")
    cells = P("normal", "span", "stream")
    return jax.shard_map(
        step, mesh=mesh, in_specs=(fields, fields, cells, fields, cells, cells, P(), P(), P()),
        out_specs=fields, check_vma=False,
    )
```

profile of v0, /device:TPU:24, one launch (start us, length us, event | category | flops | bytes accessed | tf_op | source)
XLA Modules:
  0.0 63.3 jit_solution(8827137699720200545)
XLA Ops:
  0.0 0.0 copy-start
  0.0 1.1 %copy-done = f32[5,32,8,128]{3,2,1,0:T(8,128)S(1)} copy-done((f32[5,32,8,128]{3,2,1,0:T(8,128)S(1)}, f32[5,32,8,128]{3,2,1,0:T(8,128)}, u32[]{:S(2)}) %copy-start) | copy-done | bytes 655384
  1.1 0.0 copy-start.1
  1.1 1.1 %copy-done.1 = f32[5,32,8,128]{3,2,1,0:T(8,128)S(1)} copy-done((f32[5,32,8,128]{3,2,1,0:T(8,128)S(1)}, f32[5,32,8,128]{3,2,1,0:T(8,128)}, u32[]{:S(2)}) %copy-start.1) | copy-done | bytes 655384
  2.2 0.0 copy-start.2
  2.2 1.0 %copy-done.2 = f32[3,32,8,128]{3,2,1,0:T(8,128)S(1)} copy-done((f32[3,32,8,128]{3,2,1,0:T(8,128)S(1)}, f32[3,32,8,128]{3,2,1,0:T(8,128)}, u32[]{:S(2)}) %copy-start.2) | copy-done | bytes 393240
  3.2 0.0 copy-start.3
  3.2 0.9 %copy-done.3 = f32[32,8,128]{2,1,0:T(8,128)S(1)} copy-done((f32[32,8,128]{2,1,0:T(8,128)S(1)}, f32[32,8,128]{2,1,0:T(8,128)}, u32[]{:S(2)}) %copy-start.3) | copy-done | bytes 131096
  4.1 0.0 copy-start.4
  4.1 0.9 %copy-done.4 = f32[32,8,128]{2,1,0:T(8,128)S(1)} copy-done((f32[32,8,128]{2,1,0:T(8,128)S(1)}, f32[32,8,128]{2,1,0:T(8,128)}, u32[]{:S(2)}) %copy-start.4) | copy-done | bytes 131096
  5.0 0.0 copy-start.5
  5.0 0.9 %copy-done.5 = f32[32,8,128]{2,1,0:T(8,128)S(1)} copy-done((f32[32,8,128]{2,1,0:T(8,128)S(1)}, f32[32,8,128]{2,1,0:T(8,128)}, u32[]{:S(2)}) %copy-start.5) | copy-done | bytes 131096
  5.9 0.0 copy-start.6
  5.9 0.7 %copy-done.6 = f32[5,5]{1,0:T(8,128)S(1)} copy-done((f32[5,5]{1,0:T(8,128)S(1)}, f32[5,5]{1,0:T(8,128)}, u32[]{:S(2)}) %copy-start.6) | copy-done | bytes 124
  6.6 0.0 copy-start.7
  6.6 0.7 %copy-done.7 = f32[5,5]{1,0:T(8,128)S(1)} copy-done((f32[5,5]{1,0:T(8,128)S(1)}, f32[5,5]{1,0:T(8,128)}, u32[]{:S(2)}) %copy-start.7) | copy-done | bytes 124
  7.3 0.0 copy-start.8
  7.3 0.7 %copy-done.8 = f32[5]{0:T(128)S(1)} copy-done((f32[5]{0:T(128)S(1)}, f32[5]{0:T(128)}, u32[]{:S(2)}) %copy-start.8) | copy-done | bytes 44
  7.9 54.5 %shard_map.91 = f32[5,32,8,128]{3,2,1,0:T(8,128)S(1)} custom-call(f32[5,32,8,128]{3,2,1,0:T(8,128)S(1)} %copy-done, f32[3,32,8,128]{3,2,1,0:T(8,128)S(1)} %copy-done.2, f32[32,8,128]{2,1,0:T(8,128)S(1)} %copy-done.3, f32[5,32,8,128]{3,2,1,0:T(8,128)S(1)} %copy-done.1, f32[32,8,128]{2,1,0:T(8,128)S(1)} %copy-done.4, f32[32,8,128]{2,1,0:T(8,128)S(1)} %copy-done.5, ...), custom_call_target="tpu_custom_call" | custom-call | flops 20000000 | bytes 2900000 | tf_op jit(solution)/shard_map/pallas_call | solution.py:472
  62.5 0.8 %copy.11 = f32[5,32,8,128]{3,2,1,0:T(8,128)} copy(f32[5,32,8,128]{3,2,1,0:T(8,128)S(1)} %shard_map.91) | data formatting | bytes 1310720
Async XLA Ops:
  0.0 1.1 %copy-start = (f32[5,32,8,128]{3,2,1,0:T(8,128)S(1)}, f32[5,32,8,128]{3,2,1,0:T(8,128)}, u32[]{:S(2)}) copy-start(f32[5,32,8,128]{3,2,1,0:T(8,128)} %state.1) | copy-start | bytes 1966084
  1.1 1.1 %copy-start.1 = (f32[5,32,8,128]{3,2,1,0:T(8,128)S(1)}, f32[5,32,8,128]{3,2,1,0:T(8,128)}, u32[]{:S(2)}) copy-start(f32[5,32,8,128]{3,2,1,0:T(8,128)} %source.1) | copy-start | bytes 1966084
  2.2 1.0 %copy-start.2 = (f32[3,32,8,128]{3,2,1,0:T(8,128)S(1)}, f32[3,32,8,128]{3,2,1,0:T(8,128)}, u32[]{:S(2)}) copy-start(f32[3,32,8,128]{3,2,1,0:T(8,128)} %speeds.1) | copy-start | bytes 1179652
  3.2 0.9 %copy-start.3 = (f32[32,8,128]{2,1,0:T(8,128)S(1)}, f32[32,8,128]{2,1,0:T(8,128)}, u32[]{:S(2)}) copy-start(f32[32,8,128]{2,1,0:T(8,128)} %damping.1) | copy-start | bytes 393220
  4.1 0.9 %copy-start.4 = (f32[32,8,128]{2,1,0:T(8,128)S(1)}, f32[32,8,128]{2,1,0:T(8,128)}, u32[]{:S(2)}) copy-start(f32[32,8,128]{2,1,0:T(8,128)} %nstiff.1) | copy-start | bytes 393220
  5.0 0.9 %copy-start.5 = (f32[32,8,128]{2,1,0:T(8,128)S(1)}, f32[32,8,128]{2,1,0:T(8,128)}, u32[]{:S(2)}) copy-start(f32[32,8,128]{2,1,0:T(8,128)} %wstiff.1) | copy-start | bytes 393220
  5.9 0.7 %copy-start.6 = (f32[5,5]{1,0:T(8,128)S(1)}, f32[5,5]{1,0:T(8,128)}, u32[]{:S(2)}) copy-start(f32[5,5]{1,0:T(8,128)} %left.1) | copy-start | bytes 304
  6.6 0.7 %copy-start.7 = (f32[5,5]{1,0:T(8,128)S(1)}, f32[5,5]{1,0:T(8,128)}, u32[]{:S(2)}) copy-start(f32[5,5]{1,0:T(8,128)} %right.1) | copy-start | bytes 304
  7.3 0.7 %copy-start.8 = (f32[5]{0:T(128)S(1)}, f32[5]{0:T(128)}, u32[]{:S(2)}) copy-start(f32[5]{0:T(128)} %rates.1) | copy-start | bytes 64
where the time goes:
time: 64 us; the launch traced here: 63.3 us
  Pallas kernels  54.5 us (85%)
  local copies, waits for them, and re-layouts  8.75 us (14%)
    pallas_call x1, Pallas kernels, step(): pl.pallas_call(functools.partial(kernel, nstream, nspan, nnorm), out_shap...  54.5 us
    unnamed x19, local copies, waits for them, and re-layouts  8.75 us

commit v1 on v0

--- a/solution.py
+++ b/solution.py
@@ -14,13 +14,13 @@
 
 def kernel(
     nstream, nspan, nnorm,
-    state, speeds, damping, source, nstiff, wstiff, rates, left, right,
+    state, speeds, damping, source, nstiff, wstiff, rates_in, left_in, right_in,
     out,
     st, spz, spy, spx, dmp, src, ns, ws,
     yh, xpack, xh_l, xh_r,
     inv_s, m_s, far_s, near_s, a_s, b_s, v_s,
     ab_send, ab_recv, de, pq, rc,
-    w_send, w_recv, vrow, rr_send, rr, tri, sp, xsep, o_s, consts,
+    w_send, w_recv, vrow, rr_send, rr, tri, sp, xsep, o_s, consts, rates, left, right,
     load_sem, out_sem, halo_send, halo_recv, nb_send, nb_recv,
     c_send, c_recv, r_send, r_recv, s_send, s_recv,
 ):
@@ -36,8 +36,8 @@
     at_zn, at_zp = (sx, sy, z_next), (sx, sy, z_prev)
 
     loads = [
-        (nstiff, ns), (wstiff, ws), (state, st.at[:, 2:K + 2]), (speeds.at[2], spx), (speeds.at[0], spz.at[2:K + 2]),
-        (speeds.at[1], spy), (damping, dmp), (source, src),
+        (rates_in, rates), (nstiff, ns), (wstiff, ws), (state, st.at[:, 2:K + 2]), (speeds.at[2], spx), (speeds.at[0], spz.at[2:K + 2]),
+        (speeds.at[1], spy), (damping, dmp), (source, src), (left_in, left), (right_in, right),
     ]
     load = [pltpu.make_async_copy(a, b, load_sem.at[i]) for i, (a, b) in enumerate(loads)]
     for c in load:
@@ -51,53 +51,17 @@
     def _(d):
         pl.semaphore_signal(barrier, inc=1, device_id=(sx, sy, lax.rem(sz + d, nnorm)), device_id_type=MESH)
 
-    pl.semaphore_wait(barrier, nnorm + 3)
-
     def remote(a, b, s, r, there):
         return pltpu.make_async_remote_copy(
             src_ref=a, dst_ref=b, send_sem=s, recv_sem=r, device_id=there, device_id_type=MESH
         )
 
-    halo_list = [
-        (state.at[:, :, 6:8, :], yh.at[0:NV, :, 6:8, :], at_yn),
-        (state.at[:, :, 0:2, :], yh.at[0:NV, :, 0:2, :], at_yp),
-        (speeds.at[1, :, 6:8, :], yh.at[NV, :, 6:8, :], at_yn),
-        (speeds.at[1, :, 0:2, :], yh.at[NV, :, 0:2, :], at_yp),
-        (state.at[:, K - 2:K], st.at[:, 0:2], at_zn),
-        (state.at[:, 0:2], st.at[:, K + 2:K + 4], at_zp),
-        (speeds.at[0, K - 2:K], spz.at[0:2], at_zn),
-        (speeds.at[0, 0:2], spz.at[K + 2:K + 4], at_zp),
-    ]
-    halos = [
-        remote(a, b, halo_send.at[i], halo_recv.at[i], there) for i, (a, b, there) in enumerate(halo_list)
-    ]
-    for c in halos:
-        c.start()
-
     lane = lax.broadcasted_iota(jnp.int32, (8, 128), 1)
     row = lax.broadcasted_iota(jnp.int32, (8, 128), 0)
 
-    load[2].wait()
-    load[3].wait()
-    quad = lane // 4
-
-    def pack(k, acc):
-        here = quad == k
-        tiles = [st[v, k + 2] for v in range(NV)] + [spx[k]]
-        return tuple(jnp.where(here, pltpu.roll(t, 4 * k + 2, 1), a) for t, a in zip(tiles, acc))
-
-    packed = lax.fori_loop(0, K, pack, tuple(spx[0] for _ in range(NV + 1)))
-    for i, p in enumerate(packed):
-        xpack[i] = p
-    xcopies = [
-        remote(xpack, xh_l, halo_send.at[8], halo_recv.at[8], at_xn),
-        remote(xpack, xh_r, halo_send.at[9], halo_recv.at[9], at_xp),
-    ]
-    for c in xcopies:
-        c.start()
-
     load[0].wait()
     load[1].wait()
+    load[2].wait()
     consts[0] = jnp.zeros((8, 128), F32)
     consts[1] = jnp.ones((8, 128), F32)
     zero, one = consts[0], consts[1]
@@ -149,8 +113,45 @@
         r0, r1 = done[c][0:4], done[c][4:8]
         for e, val in enumerate((r0[0], r0[1], r1[0], r1[1], r0[2], r0[3], r1[2], r1[3])):
             ab_send[e, c] = val
+    load[3].wait()
+    load[4].wait()
+    quad = lane // 4
+
+    def pack(k, acc):
+        here = quad == k
+        tiles = [st[v, k + 2] for v in range(NV)] + [spx[k]]
+        return tuple(jnp.where(here, pltpu.roll(t, 4 * k + 2, 1), a) for t, a in zip(tiles, acc))
+
+    packed = lax.fori_loop(0, K, pack, tuple(spx[0] for _ in range(NV + 1)))
+    for i, p in enumerate(packed):
+        xpack[i] = p
+    pl.semaphore_wait(barrier, nnorm + 3)
+
     ab_copy = remote(ab_send, ab_recv, nb_send.at[0], nb_recv.at[0], at_zp)
     ab_copy.start()
+
+    halo_list = [
+        (state.at[:, :, 6:8, :], yh.at[0:NV, :, 6:8, :], at_yn),
+        (state.at[:, :, 0:2, :], yh.at[0:NV, :, 0:2, :], at_yp),
+        (speeds.at[1, :, 6:8, :], yh.at[NV, :, 6:8, :], at_yn),
+        (speeds.at[1, :, 0:2, :], yh.at[NV, :, 0:2, :], at_yp),
+        (state.at[:, K - 2:K], st.at[:, 0:2], at_zn),
+        (state.at[:, 0:2], st.at[:, K + 2:K + 4], at_zp),
+        (speeds.at[0, K - 2:K], spz.at[0:2], at_zn),
+        (speeds.at[0, 0:2], spz.at[K + 2:K + 4], at_zp),
+    ]
+    halos = [
+        remote(a, b, halo_send.at[i], halo_recv.at[i], there) for i, (a, b, there) in enumerate(halo_list)
+    ]
+    for c in halos:
+        c.start()
+
+    xcopies = [
+        remote(xpack, xh_l, halo_send.at[8], halo_recv.at[8], at_xn),
+        remote(xpack, xh_r, halo_send.at[9], halo_recv.at[9], at_xp),
+    ]
+    for c in xcopies:
+        c.start()
 
     is_last = sz == nnorm - 1
     ab_copy.wait_recv()
@@ -189,45 +190,53 @@
         pq[6, c] = e10 * B00 + e11 * B10
         pq[7, c] = e10 * B01 + e11 * B11
 
-    def scatter(rows, land, s, r, t):
+    def either(t, do):
+        pl.when(t < 8)(lambda: do(0, 3))
+        pl.when(t >= 8)(lambda: do(3, 2))
+
+    def scatter(rows, land, s, r, t, first, count):
         return remote(
-            rows.at[:, pl.ds(2 * (t // 8), 3), lax.rem(t, 8), :], land.at[sz, :, 0:3, :],
+            rows.at[:, first:first + count, lax.rem(t, 8), :], land.at[sz, :, 0:count, :],
             s.at[t], r.at[sz], (sx, sy, t),
         )
 
-    def scatter_in(rows, land, s, r, t):
+    def scatter_in(rows, land, s, r, t, first, count):
         return remote(
-            rows.at[:, pl.ds(0, 3), 0, :], land.at[t, :, 0:3, :],
-            s.at[t], r.at[t], (sx, sy, t),
-        )
-
-    def scatter_own(rows, land, r):
+            rows.at[:, first:first + count, 0, :], land.at[t, :, 0:count, :], s.at[t], r.at[t], (sx, sy, t)
+        )
+
+    def scatter_own(rows, land, r, first, count):
         return pltpu.make_async_copy(
-            rows.at[:, pl.ds(2 * (sz // 8), 3), lax.rem(sz, 8), :], land.at[sz, :, 0:3, :], r.at[sz]
+            rows.at[:, first:first + count, lax.rem(sz, 8), :], land.at[sz, :, 0:count, :], r.at[sz]
         )
 
     def send_all(rows, land, s, r):
         @pl.loop(1, nnorm)
         def _(d):
-            scatter(rows, land, s, r, lax.rem(sz + d, nnorm)).start()
-
-        scatter_own(rows, land, r).start()
+            t = lax.rem(sz + d, nnorm)
+            either(t, lambda first, count: scatter(rows, land, s, r, t, first, count).start())
+
+        either(sz, lambda first, count: scatter_own(rows, land, r, first, count).start())
 
     def recv_all(rows, land, s, r):
-        @pl.loop(1, nnorm)
-        def _(d):
-            scatter_in(rows, land, s, r, lax.rem(sz + d, nnorm)).wait_recv()
-
-        scatter_own(rows, land, r).wait()
+        def every(first, count):
+            @pl.loop(1, nnorm)
+            def _(d):
+                scatter_in(rows, land, s, r, lax.rem(sz + d, nnorm), first, count).wait_recv()
+
+            scatter_own(rows, land, r, first, count).wait()
+
+        either(sz, every)
 
     def drain_all(rows, land, s, r):
         @pl.loop(1, nnorm)
         def _(d):
-            scatter(rows, land, s, r, lax.rem(sz + d, nnorm)).wait_send()
+            t = lax.rem(sz + d, nnorm)
+            either(t, lambda first, count: scatter(rows, land, s, r, t, first, count).wait_send())
 
     send_all(pq, rc, c_send, c_recv)
 
-    for c in load[4:8]:
+    for c in load[5:10]:
         c.wait()
     for c in halos:
         c.wait_recv()
@@ -323,6 +332,20 @@
     w_copy = remote(w_send, w_recv, nb_send.at[1], nb_recv.at[1], at_zp)
     w_copy.start()
 
+    w_copy.wait_recv()
+
+    @pl.when(is_last)
+    def _():
+        for c in range(NV):
+            w_recv[0, c] = zero
+            w_recv[1, c] = zero
+
+    for c in range(NV):
+        v0, v1, w0, w1 = vrow[0, c], vrow[1, c], w_recv[0, c], w_recv[1, c]
+        rr_send[0, c] = (de[0, c] * v0 + de[1, c] * v1) + (de[4, c] * w0 + de[5, c] * w1)
+        rr_send[1, c] = (de[2, c] * v0 + de[3, c] * v1) + (de[6, c] * w0 + de[7, c] * w1)
+    send_all(rr_send, rr, r_send, r_recv)
+
     recv_all(pq, rc, c_send, c_recv)
 
     def block_factor(j, carry):
@@ -347,19 +370,6 @@
 
     lax.fori_loop(0, nnorm, block_factor, (zero, zero, zero, zero))
 
-    w_copy.wait_recv()
-
-    @pl.when(is_last)
-    def _():
-        for c in range(NV):
-            w_recv[0, c] = zero
-            w_recv[1, c] = zero
-
-    for c in range(NV):
-        v0, v1, w0, w1 = vrow[0, c], vrow[1, c], w_recv[0, c], w_recv[1, c]
-        rr_send[0, c] = (de[0, c] * v0 + de[1, c] * v1) + (de[4, c] * w0 + de[5, c] * w1)
-        rr_send[1, c] = (de[2, c] * v0 + de[3, c] * v1) + (de[6, c] * w0 + de[7, c] * w1)
-    send_all(rr_send, rr, r_send, r_recv)
     recv_all(rr_send, rr, r_send, r_recv)
 
     def block_forward(j, carry):
@@ -386,37 +396,41 @@
     sp[0, 0] = zero
     sp[0, 1] = zero
 
-    def home(t):
+    def home(t, first, count):
         return remote(
-            sp.at[pl.ds(t, 2), :, 0:3, :], xsep.at[:, :, pl.ds(3 * (sz // 8), 3), lax.rem(sz, 8), :],
+            sp.at[pl.ds(t, 2), :, 0:count, :], xsep.at[:, :, first:first + count, lax.rem(sz, 8), :],
             s_send.at[t], s_recv.at[sz], (sx, sy, t),
         )
 
-    def home_in(t):
+    def home_in(t, first, count):
         return remote(
-            sp.at[pl.ds(0, 2), :, 0:3, :], xsep.at[:, :, pl.ds(3 * (t // 8), 3), lax.rem(t, 8), :],
+            sp.at[0:2, :, 0:count, :], xsep.at[:, :, first:first + count, lax.rem(t, 8), :],
             s_send.at[t], s_recv.at[t], (sx, sy, t),
         )
 
-    home_own = pltpu.make_async_copy(
-        sp.at[pl.ds(sz, 2), :, 0:3, :], xsep.at[:, :, pl.ds(3 * (sz // 8), 3), lax.rem(sz, 8), :], s_recv.at[sz]
-    )
+    def home_own(first, count):
+        return pltpu.make_async_copy(
+            sp.at[pl.ds(sz, 2), :, 0:count, :], xsep.at[:, :, first:first + count, lax.rem(sz, 8), :], s_recv.at[sz]
+        )
+
+    def home_all(first, count):
+        @pl.loop(1, nnorm)
+        def _(d):
+            home(lax.rem(sz + d, nnorm), first, count).start()
+
+        home_own(first, count).start()
+
+    either(sz, home_all)
 
     @pl.loop(1, nnorm)
     def _(d):
-        home(lax.rem(sz + d, nnorm)).start()
-
-    home_own.start()
-
-    @pl.loop(1, nnorm)
-    def _(d):
-        home_in(lax.rem(sz + d, nnorm)).wait_recv()
-
-    home_own.wait()
-
-    slot = (0, 1, 2, 4, 5)
-    pre = [(xsep[0, 0, slot[c]], xsep[0, 1, slot[c]]) for c in range(NV)]
-    own_s = [(xsep[1, 0, slot[c]], xsep[1, 1, slot[c]]) for c in range(NV)]
+        t = lax.rem(sz + d, nnorm)
+        either(t, lambda first, count: home_in(t, first, count).wait_recv())
+
+    either(sz, lambda first, count: home_own(first, count).wait())
+
+    load[10].wait()
+    own_s = [(xsep[1, 0, c], xsep[1, 1, c]) for c in range(NV)]
 
     def emit(k, xs):
         for v in range(NV):
@@ -432,15 +446,23 @@
         k = K - 3 - i
         new = []
         for c in range(NV):
-            known = v_s[c, k] + (a_s[c, k] * xsep[0, 0, slot[c]] + b_s[c, k] * xsep[0, 1, slot[c]])
+            known = v_s[c, k] + (a_s[c, k] * xsep[0, 0, c] + b_s[c, k] * xsep[0, 1, c])
             val = known + far_s[c, k] * carry[c][1] - near_s[c, k] * carry[c][0]
             new.append((val, carry[c][0]))
         emit(k, [n[0] for n in new])
         return tuple(new)
 
-    lax.fori_loop(0, K - 2, final, tuple(own_s))
-    put = pltpu.make_async_copy(o_s, out, out_sem)
-    put.start()
+    parts = 4
+    rows = K // parts
+    carry, begin = tuple(own_s), 0
+    puts = []
+    for p in reversed(range(parts)):
+        stop = K - 2 - p * rows
+        carry = lax.fori_loop(begin, stop, final, carry)
+        begin = stop
+        put = pltpu.make_async_copy(o_s.at[:, p * rows:(p + 1) * rows], out.at[:, p * rows:(p + 1) * rows], out_sem.at[p])
+        put.start()
+        puts.append(put)
 
     for c in halos:
         c.wait_send()
@@ -451,11 +473,14 @@
     drain_all(pq, rc, c_send, c_recv)
     drain_all(rr_send, rr, r_send, r_recv)
 
-    @pl.loop(1, nnorm)
-    def _(d):
-        home(lax.rem(sz + d, nnorm)).wait_send()
-
-    put.wait()
+    def home_drain(first, count):
+        @pl.loop(1, nnorm)
+        def _(d):
+            home(lax.rem(sz + d, nnorm), first, count).wait_send()
+
+    either(sz, home_drain)
+    for put in puts:
+        put.wait()
 
 
 def solution(mesh):
@@ -467,12 +492,11 @@
         vm = lambda *s: pltpu.VMEM(s + T, F32)
         dma = lambda n: pltpu.SemaphoreType.DMA((n,))
         hbm = pl.BlockSpec(memory_space=pltpu.HBM)
-        smem = pl.BlockSpec(memory_space=pltpu.SMEM)
         per = lambda: vm(NV, K)
         return pl.pallas_call(
             functools.partial(kernel, nstream, nspan, nnorm),
             out_shape=jax.ShapeDtypeStruct(state.shape, F32),
-            in_specs=[hbm] * 6 + [smem] * 3,
+            in_specs=[hbm] * 9,
             out_specs=hbm,
             scratch_shapes=[
                 vm(NV, K + 4), vm(K + 4), vm(K), vm(K), vm(K), vm(NV, K), vm(K), vm(K),
@@ -480,12 +504,13 @@
                 per(), per(), per(), per(), per(), per(), per(),
                 vm(8, NV), vm(8, NV), vm(8, NV), vm(8, NV), vm(nnorm, 8),
                 vm(2, NV), vm(2, NV), vm(2, NV), vm(2, NV), vm(nnorm, 2), vm(nnorm, 12), vm(nnorm + 1, 2),
-                vm(2, 2, 6), vm(NV, K), vm(2),
-                dma(8), pltpu.SemaphoreType.DMA, dma(10), dma(10), dma(2), dma(2),
+                vm(2, 2, NV), vm(NV, K), vm(2),
+                pltpu.SMEM((NV,), F32), pltpu.SMEM((NV, NV), F32), pltpu.SMEM((NV, NV), F32),
+                dma(11), dma(4), dma(10), dma(10), dma(2), dma(2),
                 dma(nnorm), dma(nnorm), dma(nnorm), dma(nnorm), dma(nnorm), dma(nnorm),
             ],
             compiler_params=pltpu.CompilerParams(
-                collective_id=0, has_side_effects=True, vmem_limit_bytes=32 * 1024 * 1024
+                collective_id=0, has_side_effects=True, vmem_limit_bytes=60 * 1024 * 1024
             ),
             cost_estimate=pl.CostEstimate(flops=20_000_000, bytes_accessed=2_900_000, transcendentals=0),
         )(state, speeds, damping, source, normal_stiff, wide_stiff, char_rates, left_vectors, right_vectors)

time: 64 us -> 49.9 us (0.78)
  Pallas kernels: 54.5 us -> 47.6 us
  local copies, waits for them, and re-layouts: 8.75 us -> 1.97 us
    pallas_call x1, Pallas kernels: 54.5 us -> 47.6 us  [step(): pl.pallas_call(functools.partial(kernel, nstream, nspan, nnorm), out_shap...]
    unnamed x19 -> x1, local copies, waits for them, and re-layouts: 8.75 us -> 1.97 us
where the time goes in v1:
time: 49.9 us; the launch traced here: 49.6 us
  Pallas kernels  47.6 us (95%)
  local copies, waits for them, and re-layouts  1.97 us (4%)
    pallas_call x1, Pallas kernels, step(): pl.pallas_call(functools.partial(kernel, nstream, nspan, nnorm), out_shap...  47.6 us
    unnamed x1, local copies, waits for them, and re-layouts  1.97 us

profile of v1, /device:TPU:24, one launch (start us, length us, event | category | flops | bytes accessed | tf_op | source)
XLA Modules:
  0.0 49.6 jit_solution(15332166190157204690)
XLA Ops:
  0.0 47.6 %shard_map.91 = f32[5,32,8,128]{3,2,1,0:T(8,128)} custom-call(f32[5,32,8,128]{3,2,1,0:T(8,128)} %state.1, f32[3,32,8,128]{3,2,1,0:T(8,128)} %speeds.1, f32[32,8,128]{2,1,0:T(8,128)} %damping.1, f32[5,32,8,128]{3,2,1,0:T(8,128)} %source.1, f32[32,8,128]{2,1,0:T(8,128)} %nstiff.1, f32[32,8,128]{2,1,0:T(8,128)} %wstiff.1, f32[5]{0:T(128)} %rates_in.1, ...), custom_call_target="tpu_custom_call" | custom-call | flops 20000000 | bytes 2900000 | tf_op jit(solution)/shard_map/pallas_call | solution.py:496
  47.6 2.0 %copy.11 = f32[5,32,8,128]{3,2,1,0:T(8,128)} copy(f32[5,32,8,128]{3,2,1,0:T(8,128)} %shard_map.91) | data formatting | bytes 1310720

commit v2 on v1

--- a/solution.py
+++ b/solution.py
@@ -19,9 +19,9 @@
     st, spz, spy, spx, dmp, src, ns, ws,
     yh, xpack, xh_l, xh_r,
     inv_s, m_s, far_s, near_s, a_s, b_s, v_s,
-    ab_send, ab_recv, de, pq, rc,
-    w_send, w_recv, vrow, rr_send, rr, tri, sp, xsep, o_s, consts, rates, left, right,
-    load_sem, out_sem, halo_send, halo_recv, nb_send, nb_recv,
+    a_send, a_recv, n_send, n_recv, spike, de, pq, rc,
+    rr_send, rr, tri, sp, xsep, consts, rates, left, right,
+    load_sem, halo_send, halo_recv, nb_send, nb_recv,
     c_send, c_recv, r_send, r_recv, s_send, s_recv,
 ):
     K = nstiff.shape[0]
@@ -111,8 +111,18 @@
     done = lax.fori_loop(0, K - 2, spikes, tuple(start for _ in range(NV)))
     for c in range(NV):
         r0, r1 = done[c][0:4], done[c][4:8]
-        for e, val in enumerate((r0[0], r0[1], r1[0], r1[1], r0[2], r0[3], r1[2], r1[3])):
-            ab_send[e, c] = val
+        for e, val in enumerate((r0[0], r0[1], r1[0], r1[1])):
+            a_send[e, c] = val
+        for e, val in enumerate((r0[2], r0[3], r1[2], r1[3])):
+            spike[e, c] = val
+        n30, n31, h30, h31 = near_s[c, K - 2], near_s[c, K - 1], far_s[c, K - 2], far_s[c, K - 1]
+        for e, val in enumerate((n30 * n31 + h30, -n30 * h31, -n31, h31)):
+            n_send[e, c] = val
+    for e in range(4):
+        rc[nnorm, 4 + e] = zero
+    for e in range(2):
+        rr[nnorm, 2 + e] = zero
+
     load[3].wait()
     load[4].wait()
     quad = lane // 4
@@ -126,9 +136,6 @@
     for i, p in enumerate(packed):
         xpack[i] = p
     pl.semaphore_wait(barrier, nnorm + 3)
-
-    ab_copy = remote(ab_send, ab_recv, nb_send.at[0], nb_recv.at[0], at_zp)
-    ab_copy.start()
 
     halo_list = [
         (state.at[:, :, 6:8, :], yh.at[0:NV, :, 6:8, :], at_yn),
@@ -153,42 +160,51 @@
     for c in xcopies:
         c.start()
 
+    nb = [
+        remote(a_send, a_recv, nb_send.at[0], nb_recv.at[0], at_zp),
+        remote(n_send, n_recv, nb_send.at[1], nb_recv.at[1], at_zn),
+    ]
+    for c in nb:
+        c.start()
+    for c in nb:
+        c.wait_recv()
+
     is_last = sz == nnorm - 1
-    ab_copy.wait_recv()
 
     @pl.when(is_last)
     def _():
-        @pl.loop(0, 8)
-        def _(e):
+        for e in range(4):
             for c in range(NV):
-                ab_recv[e, c] = zero
+                a_recv[e, c] = zero
+
+    def inverse(n, a):
+        m00 = 1.0 - (n[0] * a[0] + n[1] * a[2])
+        m01 = -(n[0] * a[1] + n[1] * a[3])
+        m10 = -(n[2] * a[0] + n[3] * a[2])
+        m11 = 1.0 - (n[2] * a[1] + n[3] * a[3])
+        det = 1.0 / (m00 * m11 - m01 * m10)
+        return m11 * det, -m01 * det, -m10 * det, m00 * det
+
+    def times(p, q):
+        return (
+            p[0] * q[0] + p[1] * q[2], p[0] * q[1] + p[1] * q[3],
+            p[2] * q[0] + p[3] * q[2], p[2] * q[1] + p[3] * q[3],
+        )
 
     @pl.loop(0, NV)
     def _(c):
-        n30, n31, h30, h31 = near_s[c, K - 2], near_s[c, K - 1], far_s[c, K - 2], far_s[c, K - 1]
-        a30, a31, b30, b31 = a_s[c, K - 2], a_s[c, K - 1], b_s[c, K - 2], b_s[c, K - 1]
-        n00, n01, n10, n11 = n30 * n31 + h30, -n30 * h31, -n31, h31
-        s00, s01, s10, s11 = a30 - n30 * a31, b30 - n30 * b31, a31, b31
-        A00, A01, A10, A11 = ab_recv[0, c], ab_recv[1, c], ab_recv[2, c], ab_recv[3, c]
-        B00, B01, B10, B11 = ab_recv[4, c], ab_recv[5, c], ab_recv[6, c], ab_recv[7, c]
-        m00 = 1.0 - (n00 * A00 + n01 * A10)
-        m01 = -(n00 * A01 + n01 * A11)
-        m10 = -(n10 * A00 + n11 * A10)
-        m11 = 1.0 - (n10 * A01 + n11 * A11)
-        det = 1.0 / (m00 * m11 - m01 * m10)
-        d00, d01, d10, d11 = m11 * det, -m01 * det, -m10 * det, m00 * det
-        e00, e01 = d00 * n00 + d01 * n10, d00 * n01 + d01 * n11
-        e10, e11 = d10 * n00 + d11 * n10, d10 * n01 + d11 * n11
-        for i, val in enumerate((d00, d01, d10, d11, e00, e01, e10, e11)):
-            de[i, c] = val
-        pq[0, c] = d00 * s00 + d01 * s10
-        pq[1, c] = d00 * s01 + d01 * s11
-        pq[2, c] = d10 * s00 + d11 * s10
-        pq[3, c] = d10 * s01 + d11 * s11
-        pq[4, c] = e00 * B00 + e01 * B10
-        pq[5, c] = e00 * B01 + e01 * B11
-        pq[6, c] = e10 * B00 + e11 * B10
-        pq[7, c] = e10 * B01 + e11 * B11
+        four = lambda ref: tuple(ref[e, c] for e in range(4))
+        n30, a30, a31, b30, b31 = near_s[c, K - 2], a_s[c, K - 2], a_s[c, K - 1], b_s[c, K - 2], b_s[c, K - 1]
+        d = inverse(four(n_send), four(a_recv))
+        p = times(d, (a30 - n30 * a31, b30 - n30 * b31, a31, b31))
+        before = four(n_recv)
+        e_ = times(inverse(before, four(a_send)), before)
+        q = times(e_, four(spike))
+        for i in range(4):
+            de[i, c] = d[i]
+            de[4 + i, c] = e_[i]
+            pq[i, c] = p[i]
+            pq[4 + i, c] = q[i]
 
     def either(t, do):
         pl.when(t < 8)(lambda: do(0, 3))
@@ -210,10 +226,13 @@
             rows.at[:, first:first + count, lax.rem(sz, 8), :], land.at[sz, :, 0:count, :], r.at[sz]
         )
 
+    def peer(i):
+        return lax.rem(sz + nnorm // 2 + ((i + 1) // 2) * (1 - 2 * lax.rem(i, 2)), nnorm)
+
     def send_all(rows, land, s, r):
-        @pl.loop(1, nnorm)
-        def _(d):
-            t = lax.rem(sz + d, nnorm)
+        @pl.loop(0, nnorm - 1)
+        def _(i):
+            t = peer(i)
             either(t, lambda first, count: scatter(rows, land, s, r, t, first, count).start())
 
         either(sz, lambda first, count: scatter_own(rows, land, r, first, count).start())
@@ -324,49 +343,25 @@
 
     firsts = lax.fori_loop(0, K - 2, back, tuple((zero, zero) for _ in range(NV)))
     for c in range(NV):
-        w_send[0, c] = firsts[c][0]
-        w_send[1, c] = firsts[c][1]
-        v31, v30 = ends[c]
-        vrow[0, c] = v30 - near_s[c, K - 2] * v31
-        vrow[1, c] = v31
-    w_copy = remote(w_send, w_recv, nb_send.at[1], nb_recv.at[1], at_zp)
-    w_copy.start()
-
-    w_copy.wait_recv()
-
-    @pl.when(is_last)
-    def _():
-        for c in range(NV):
-            w_recv[0, c] = zero
-            w_recv[1, c] = zero
-
-    for c in range(NV):
-        v0, v1, w0, w1 = vrow[0, c], vrow[1, c], w_recv[0, c], w_recv[1, c]
-        rr_send[0, c] = (de[0, c] * v0 + de[1, c] * v1) + (de[4, c] * w0 + de[5, c] * w1)
-        rr_send[1, c] = (de[2, c] * v0 + de[3, c] * v1) + (de[6, c] * w0 + de[7, c] * w1)
+        w0, w1 = firsts[c]
+        v1 = ends[c][0]
+        v0 = ends[c][1] - near_s[c, K - 2] * v1
+        rr_send[0, c] = de[0, c] * v0 + de[1, c] * v1
+        rr_send[1, c] = de[2, c] * v0 + de[3, c] * v1
+        rr_send[2, c] = de[4, c] * w0 + de[5, c] * w1
+        rr_send[3, c] = de[6, c] * w0 + de[7, c] * w1
     send_all(rr_send, rr, r_send, r_recv)
 
     recv_all(pq, rc, c_send, c_recv)
 
     def block_factor(j, carry):
-        t00, t01, t10, t11 = carry
-        p00, p01, p10, p11, q00, q01, q10, q11 = [rc[j, e] for e in range(8)]
-        m00 = 1.0 - (p00 * t00 + p01 * t10)
-        m01 = -(p00 * t01 + p01 * t11)
-        m10 = -(p10 * t00 + p11 * t10)
-        m11 = 1.0 - (p10 * t01 + p11 * t11)
-        det = 1.0 / (m00 * m11 - m01 * m10)
-        d00, d01, d10, d11 = m11 * det, -m01 * det, -m10 * det, m00 * det
-        t00, t01 = d00 * q00 + d01 * q10, d00 * q01 + d01 * q11
-        t10, t11 = d10 * q00 + d11 * q10, d10 * q01 + d11 * q11
-        vals = (
-            d00, d01, d10, d11,
-            d00 * p00 + d01 * p10, d00 * p01 + d01 * p11, d10 * p00 + d11 * p10, d10 * p01 + d11 * p11,
-            t00, t01, t10, t11,
-        )
-        for i, val in enumerate(vals):
+        p = tuple(rc[j, e] for e in range(4))
+        q = tuple(rc[j + 1, 4 + e] for e in range(4))
+        d = inverse(p, carry)
+        t = times(d, q)
+        for i, val in enumerate(d + times(d, p) + t):
             tri[j, i] = val
-        return (t00, t01, t10, t11)
+        return t
 
     lax.fori_loop(0, nnorm, block_factor, (zero, zero, zero, zero))
 
@@ -374,7 +369,7 @@
 
     def block_forward(j, carry):
         z0, z1 = carry
-        r0, r1 = rr[j, 0], rr[j, 1]
+        r0, r1 = rr[j, 0] + rr[j + 1, 2], rr[j, 1] + rr[j + 1, 3]
         n0 = (tri[j, 0] * r0 + tri[j, 1] * r1) + (tri[j, 4] * z0 + tri[j, 5] * z1)
         n1 = (tri[j, 2] * r0 + tri[j, 3] * r1) + (tri[j, 6] * z0 + tri[j, 7] * z1)
         rr[j, 0] = n0
@@ -414,9 +409,9 @@
         )
 
     def home_all(first, count):
-        @pl.loop(1, nnorm)
-        def _(d):
-            home(lax.rem(sz + d, nnorm), first, count).start()
+        @pl.loop(0, nnorm - 1)
+        def _(i):
+            home(peer(i), first, count).start()
 
         home_own(first, count).start()
 
@@ -437,7 +432,7 @@
             u = right[v, 0] * xs[0]
             for c in range(1, NV):
                 u = u + right[v, c] * xs[c]
-            o_s[v, k] = u
+            out[v, k] = u
 
     emit(K - 1, [s[1] for s in own_s])
     emit(K - 2, [s[0] for s in own_s])
@@ -452,24 +447,14 @@
         emit(k, [n[0] for n in new])
         return tuple(new)
 
-    parts = 4
-    rows = K // parts
-    carry, begin = tuple(own_s), 0
-    puts = []
-    for p in reversed(range(parts)):
-        stop = K - 2 - p * rows
-        carry = lax.fori_loop(begin, stop, final, carry)
-        begin = stop
-        put = pltpu.make_async_copy(o_s.at[:, p * rows:(p + 1) * rows], out.at[:, p * rows:(p + 1) * rows], out_sem.at[p])
-        put.start()
-        puts.append(put)
+    lax.fori_loop(0, K - 2, final, tuple(own_s))
 
     for c in halos:
         c.wait_send()
     for c in xcopies:
         c.wait_send()
-    ab_copy.wait_send()
-    w_copy.wait_send()
+    for c in nb:
+        c.wait_send()
     drain_all(pq, rc, c_send, c_recv)
     drain_all(rr_send, rr, r_send, r_recv)
 
@@ -479,8 +464,6 @@
             home(lax.rem(sz + d, nnorm), first, count).wait_send()
 
     either(sz, home_drain)
-    for put in puts:
-        put.wait()
 
 
 def solution(mesh):
@@ -495,18 +478,17 @@
         per = lambda: vm(NV, K)
         return pl.pallas_call(
             functools.partial(kernel, nstream, nspan, nnorm),
-            out_shape=jax.ShapeDtypeStruct(state.shape, F32),
+            out_shape=pltpu.VMEM(state.shape, F32),
             in_specs=[hbm] * 9,
-            out_specs=hbm,
+            out_specs=pl.BlockSpec(memory_space=pltpu.VMEM),
             scratch_shapes=[
                 vm(NV, K + 4), vm(K + 4), vm(K), vm(K), vm(K), vm(NV, K), vm(K), vm(K),
                 vm(NV + 1, K), vm(NV + 1), vm(NV + 1), vm(NV + 1),
                 per(), per(), per(), per(), per(), per(), per(),
-                vm(8, NV), vm(8, NV), vm(8, NV), vm(8, NV), vm(nnorm, 8),
-                vm(2, NV), vm(2, NV), vm(2, NV), vm(2, NV), vm(nnorm, 2), vm(nnorm, 12), vm(nnorm + 1, 2),
-                vm(2, 2, NV), vm(NV, K), vm(2),
+                vm(4, NV), vm(4, NV), vm(4, NV), vm(4, NV), vm(4, NV), vm(8, NV), vm(8, NV), vm(nnorm + 1, 8),
+                vm(4, NV), vm(nnorm + 1, 4), vm(nnorm, 12), vm(nnorm + 1, 2), vm(2, 2, NV), vm(2),
                 pltpu.SMEM((NV,), F32), pltpu.SMEM((NV, NV), F32), pltpu.SMEM((NV, NV), F32),
-                dma(11), dma(4), dma(10), dma(10), dma(2), dma(2),
+                dma(11), dma(10), dma(10), dma(2), dma(2),
                 dma(nnorm), dma(nnorm), dma(nnorm), dma(nnorm), dma(nnorm), dma(nnorm),
             ],
             compiler_params=pltpu.CompilerParams(

time: 49.9 us -> 45.7 us (0.916)
  Pallas kernels: 47.6 us -> 44.5 us
  local copies, waits for them, and re-layouts: 1.97 us -> 0.84 us
    pallas_call x1, Pallas kernels: 47.6 us -> 44.5 us  [step(): pl.pallas_call(functools.partial(kernel, nstream, nspan, nnorm), out_shap...]
    unnamed x1, local copies, waits for them, and re-layouts: 1.97 us -> 0.84 us
where the time goes in v2:
time: 45.7 us; the launch traced here: 45.4 us
  Pallas kernels  44.5 us (97%)
  local copies, waits for them, and re-layouts  0.84 us (2%)
    pallas_call x1, Pallas kernels, step(): pl.pallas_call(functools.partial(kernel, nstream, nspan, nnorm), out_shap...  44.5 us

profile of v2, /device:TPU:24, one launch (start us, length us, event | category | flops | bytes accessed | tf_op | source)
XLA Modules:
  0.0 45.4 jit_solution(14279490808691367956)
XLA Ops:
  0.0 44.5 %shard_map.91 = f32[5,32,8,128]{3,2,1,0:T(8,128)S(1)} custom-call(f32[5,32,8,128]{3,2,1,0:T(8,128)} %state.1, f32[3,32,8,128]{3,2,1,0:T(8,128)} %speeds.1, f32[32,8,128]{2,1,0:T(8,128)} %damping.1, f32[5,32,8,128]{3,2,1,0:T(8,128)} %source.1, f32[32,8,128]{2,1,0:T(8,128)} %nstiff.1, f32[32,8,128]{2,1,0:T(8,128)} %wstiff.1, f32[5]{0:T(128)} %rates_in.1, ...), custom_call_target="tpu_custom_call" | custom-call | flops 20000000 | bytes 2900000 | tf_op jit(solution)/shard_map/pallas_call | solution.py:479
  44.5 0.8 %copy.11 = f32[5,32,8,128]{3,2,1,0:T(8,128)} copy(f32[5,32,8,128]{3,2,1,0:T(8,128)S(1)} %shard_map.91) | data formatting | bytes 1310720

commit v3 on v2

--- a/solution.py
+++ b/solution.py
@@ -12,12 +12,21 @@
 F32 = jnp.float32
 
 
+def loop(begin, end, body, carry, unroll):
+    def several(i, carry):
+        for j in range(unroll):
+            carry = body(begin + i * unroll + j, carry)
+        return carry
+
+    return lax.fori_loop(0, (end - begin) // unroll, several, carry)
+
+
 def kernel(
     nstream, nspan, nnorm,
     state, speeds, damping, source, nstiff, wstiff, rates_in, left_in, right_in,
     out,
     st, spz, spy, spx, dmp, src, ns, ws,
-    yh, xpack, xh_l, xh_r,
+    yh, zh_p, zh_n, xpack, xh_l, xh_r, xcor,
     inv_s, m_s, far_s, near_s, a_s, b_s, v_s,
     a_send, a_recv, n_send, n_recv, spike, de, pq, rc,
     rr_send, rr, tri, sp, xsep, consts, rates, left, right,
@@ -35,21 +44,24 @@
     at_yn, at_yp = (sx, y_next, sz), (sx, y_prev, sz)
     at_zn, at_zp = (sx, sy, z_next), (sx, sy, z_prev)
 
+    barrier = pltpu.get_barrier_semaphore()
+    def peer(i):
+        return lax.rem(sz + nnorm // 2 + ((i + 1) // 2) * (1 - 2 * lax.rem(i, 2)), nnorm)
+
+    @pl.loop(0, nnorm - 1)
+    def _(i):
+        pl.semaphore_signal(barrier, inc=1, device_id=(sx, sy, peer(i)), device_id_type=MESH)
+
+    for there in (at_xn, at_xp, at_yn, at_yp):
+        pl.semaphore_signal(barrier, inc=1, device_id=there, device_id_type=MESH)
+
     loads = [
-        (rates_in, rates), (nstiff, ns), (wstiff, ws), (state, st.at[:, 2:K + 2]), (speeds.at[2], spx), (speeds.at[0], spz.at[2:K + 2]),
-        (speeds.at[1], spy), (damping, dmp), (source, src), (left_in, left), (right_in, right),
+        (rates_in, rates), (nstiff, ns), (wstiff, ws), (state, st.at[:, 2:K + 2]), (speeds.at[2], spx), (damping, dmp),
+        (speeds.at[0], spz.at[2:K + 2]), (speeds.at[1], spy), (source, src), (left_in, left), (right_in, right),
     ]
     load = [pltpu.make_async_copy(a, b, load_sem.at[i]) for i, (a, b) in enumerate(loads)]
     for c in load:
         c.start()
-
-    barrier = pltpu.get_barrier_semaphore()
-    for there in (at_xn, at_xp, at_yn, at_yp):
-        pl.semaphore_signal(barrier, inc=1, device_id=there, device_id_type=MESH)
-
-    @pl.loop(1, nnorm)
-    def _(d):
-        pl.semaphore_signal(barrier, inc=1, device_id=(sx, sy, lax.rem(sz + d, nnorm)), device_id_type=MESH)
 
     def remote(a, b, s, r, there):
         return pltpu.make_async_remote_copy(
@@ -118,6 +130,16 @@
         n30, n31, h30, h31 = near_s[c, K - 2], near_s[c, K - 1], far_s[c, K - 2], far_s[c, K - 1]
         for e, val in enumerate((n30 * n31 + h30, -n30 * h31, -n31, h31)):
             n_send[e, c] = val
+    for k in (0, 1, K + 2, K + 3):
+        spz[k] = zero
+        for v in range(NV):
+            st[v, k] = zero
+
+    @pl.loop(0, K)
+    def _(k):
+        for v in range(NV + 1):
+            yh[v, k, 2:6] = jnp.zeros((4, 128), F32)
+
     for e in range(4):
         rc[nnorm, 4 + e] = zero
     for e in range(2):
@@ -125,27 +147,35 @@
 
     load[3].wait()
     load[4].wait()
+    load[5].wait()
     quad = lane // 4
 
     def pack(k, acc):
         here = quad == k
-        tiles = [st[v, k + 2] for v in range(NV)] + [spx[k]]
+        tiles = [st[v, k + 2] for v in range(NV)] + [spx[k], dmp[k]]
         return tuple(jnp.where(here, pltpu.roll(t, 4 * k + 2, 1), a) for t, a in zip(tiles, acc))
 
-    packed = lax.fori_loop(0, K, pack, tuple(spx[0] for _ in range(NV + 1)))
+    packed = lax.fori_loop(0, K, pack, tuple(spx[0] for _ in range(NV + 2)))
     for i, p in enumerate(packed):
         xpack[i] = p
     pl.semaphore_wait(barrier, nnorm + 3)
 
+    nb = [
+        remote(a_send, a_recv, nb_send.at[0], nb_recv.at[0], at_zp),
+        remote(n_send, n_recv, nb_send.at[1], nb_recv.at[1], at_zn),
+    ]
+    for c in nb:
+        c.start()
+
     halo_list = [
-        (state.at[:, :, 6:8, :], yh.at[0:NV, :, 6:8, :], at_yn),
-        (state.at[:, :, 0:2, :], yh.at[0:NV, :, 0:2, :], at_yp),
-        (speeds.at[1, :, 6:8, :], yh.at[NV, :, 6:8, :], at_yn),
-        (speeds.at[1, :, 0:2, :], yh.at[NV, :, 0:2, :], at_yp),
-        (state.at[:, K - 2:K], st.at[:, 0:2], at_zn),
-        (state.at[:, 0:2], st.at[:, K + 2:K + 4], at_zp),
-        (speeds.at[0, K - 2:K], spz.at[0:2], at_zn),
-        (speeds.at[0, 0:2], spz.at[K + 2:K + 4], at_zp),
+        (state.at[:, :, 6:8, :], yh.at[0:NV, :, 0:2, :], at_yn),
+        (state.at[:, :, 0:2, :], yh.at[0:NV, :, 6:8, :], at_yp),
+        (speeds.at[1, :, 6:8, :], yh.at[NV, :, 0:2, :], at_yn),
+        (speeds.at[1, :, 0:2, :], yh.at[NV, :, 6:8, :], at_yp),
+        (state.at[:, K - 2:K], zh_p.at[0:NV], at_zn),
+        (state.at[:, 0:2], zh_n.at[0:NV], at_zp),
+        (speeds.at[0, K - 2:K], zh_p.at[NV], at_zn),
+        (speeds.at[0, 0:2], zh_n.at[NV], at_zp),
     ]
     halos = [
         remote(a, b, halo_send.at[i], halo_recv.at[i], there) for i, (a, b, there) in enumerate(halo_list)
@@ -154,18 +184,46 @@
         c.start()
 
     xcopies = [
-        remote(xpack, xh_l, halo_send.at[8], halo_recv.at[8], at_xn),
-        remote(xpack, xh_r, halo_send.at[9], halo_recv.at[9], at_xp),
+        remote(xpack.at[0:NV + 1], xh_l, halo_send.at[8], halo_recv.at[8], at_xn),
+        remote(xpack.at[0:NV + 1], xh_r, halo_send.at[9], halo_recv.at[9], at_xp),
     ]
     for c in xcopies:
         c.start()
 
-    nb = [
-        remote(a_send, a_recv, nb_send.at[0], nb_recv.at[0], at_zp),
-        remote(n_send, n_recv, nb_send.at[1], nb_recv.at[1], at_zn),
-    ]
-    for c in nb:
-        c.start()
+    for c in load[6:9]:
+        c.wait()
+    C1, C2 = 2.0 / 3.0, 1.0 / 12.0
+    x_in = (lane < 127, lane < 126, lane > 0, lane > 1)
+    y_in = (row < 7, row < 6, row > 0, row > 1)
+
+    def around(t, size, axis):
+        return tuple(pltpu.roll(t, shift, axis) for shift in (size - 1, size - 2, 1, 2))
+
+    def interior(k, carry):
+        d = dmp[k]
+        d4 = 4.0 * d
+
+        def weights(p1, p2, m1, m2):
+            return d4 - C1 * p1, C2 * p2 - d, d4 + C1 * m1, -d - C2 * m2
+
+        wx = [jnp.where(i, w, 0.0) for i, w in zip(x_in, weights(*around(spx[k], 128, 1)))]
+        wy = [jnp.where(i, w, 0.0) for i, w in zip(y_in, weights(*around(spy[k], 8, 0)))]
+        wz = weights(spz[k + 3], spz[k + 4], spz[k + 1], spz[k])
+        wc = -18.0 * d
+        for v in range(NV):
+            t = st[v, k + 2]
+            acc = src[v, k] + wc * t
+            zs = (st[v, k + 3], st[v, k + 4], st[v, k + 1], st[v, k])
+            accz = wz[0] * zs[0] + wz[1] * zs[1] + wz[2] * zs[2] + wz[3] * zs[3]
+            xs = around(t, 128, 1)
+            accx = wx[0] * xs[0] + wx[1] * xs[1] + wx[2] * xs[2] + wx[3] * xs[3]
+            ys = around(t, 8, 0)
+            accy = wy[0] * ys[0] + wy[1] * ys[1] + wy[2] * ys[2] + wy[3] * ys[3]
+            src[v, k] = (acc + accz) + (accx + accy)
+        return carry
+
+    lax.fori_loop(0, K // 4, interior, 0)
+
     for c in nb:
         c.wait_recv()
 
@@ -191,9 +249,8 @@
             p[2] * q[0] + p[3] * q[2], p[2] * q[1] + p[3] * q[3],
         )
 
-    @pl.loop(0, NV)
-    def _(c):
-        four = lambda ref: tuple(ref[e, c] for e in range(4))
+    for c in range(NV):
+        four = lambda ref, c=c: tuple(ref[e, c] for e in range(4))
         n30, a30, a31, b30, b31 = near_s[c, K - 2], a_s[c, K - 2], a_s[c, K - 1], b_s[c, K - 2], b_s[c, K - 1]
         d = inverse(four(n_send), four(a_recv))
         p = times(d, (a30 - n30 * a31, b30 - n30 * b31, a31, b31))
@@ -206,13 +263,19 @@
             pq[i, c] = p[i]
             pq[4 + i, c] = q[i]
 
+    def heavy(t):
+        return lax.rem(t, 2) == 0
+
+    def line(t):
+        return t // 2
+
     def either(t, do):
-        pl.when(t < 8)(lambda: do(0, 3))
-        pl.when(t >= 8)(lambda: do(3, 2))
+        pl.when(heavy(t))(lambda: do(0, 3))
+        pl.when(jnp.logical_not(heavy(t)))(lambda: do(3, 2))
 
     def scatter(rows, land, s, r, t, first, count):
         return remote(
-            rows.at[:, first:first + count, lax.rem(t, 8), :], land.at[sz, :, 0:count, :],
+            rows.at[:, first:first + count, line(t), :], land.at[sz, :, 0:count, :],
             s.at[t], r.at[sz], (sx, sy, t),
         )
 
@@ -223,11 +286,8 @@
 
     def scatter_own(rows, land, r, first, count):
         return pltpu.make_async_copy(
-            rows.at[:, first:first + count, lax.rem(sz, 8), :], land.at[sz, :, 0:count, :], r.at[sz]
-        )
-
-    def peer(i):
-        return lax.rem(sz + nnorm // 2 + ((i + 1) // 2) * (1 - 2 * lax.rem(i, 2)), nnorm)
+            rows.at[:, first:first + count, line(sz), :], land.at[sz, :, 0:count, :], r.at[sz]
+        )
 
     def send_all(rows, land, s, r):
         @pl.loop(0, nnorm - 1)
@@ -255,73 +315,79 @@
 
     send_all(pq, rc, c_send, c_recv)
 
-    for c in load[5:10]:
+    lax.fori_loop(K // 4, K, interior, 0)
+
+    for c in load[9:10]:
         c.wait()
     for c in halos:
         c.wait_recv()
     for c in xcopies:
         c.wait_recv()
 
-    @pl.when(sz == 0)
+    @pl.when(sz > 0)
     def _():
+        d0, d1, a0, a1 = dmp[0], dmp[1], zh_p[NV, 0], zh_p[NV, 1]
+        w02, w01, w12 = -d0 - C2 * a0, 4.0 * d0 + C1 * a1, -d1 - C2 * a1
         for v in range(NV):
-            st[v, 0] = zero
-            st[v, 1] = zero
-
-    @pl.when(is_last)
+            src[v, 0] = src[v, 0] + (w02 * zh_p[v, 0] + w01 * zh_p[v, 1])
+            src[v, 1] = src[v, 1] + w12 * zh_p[v, 1]
+
+    @pl.when(sz < nnorm - 1)
     def _():
+        d0, d1, a0, a1 = dmp[K - 1], dmp[K - 2], zh_n[NV, 0], zh_n[NV, 1]
+        w01, w02, w12 = 4.0 * d0 - C1 * a0, C2 * a1 - d0, C2 * a0 - d1
         for v in range(NV):
-            st[v, K + 2] = zero
-            st[v, K + 3] = zero
-
-    take_left = lax.rem(lane, 4) < 2
-    for i in range(NV + 1):
-        xpack_h = jnp.where(take_left, xh_l[i], xh_r[i])
-        xh_l[i] = xpack_h
-
-    def gate(inside, ok):
-        return jnp.where(inside, one, jnp.where(ok, 1.0, 0.0).astype(F32) * one)
-
-    has_xn, has_xp = sx < nstream - 1, sx > 0
-    has_yn, has_yp = sy < nspan - 1, sy > 0
-    gx_p1, gx_p2 = gate(lane < 127, has_xn), gate(lane < 126, has_xn)
-    gx_m1, gx_m2 = gate(lane > 0, has_xp), gate(lane > 1, has_xp)
-    gy_p1, gy_p2 = gate(row < 7, has_yn), gate(row < 6, has_yn)
-    gy_m1, gy_m2 = gate(row > 0, has_yp), gate(row > 1, has_yp)
-
-    def around(t, h, index, size, axis):
+            src[v, K - 1] = src[v, K - 1] + (w01 * zh_n[v, 0] + w02 * zh_n[v, 1])
+            src[v, K - 2] = src[v, K - 2] + w12 * zh_n[v, 0]
+
+    def number(yes):
+        return jnp.where(yes, 1.0, 0.0).astype(F32)
+
+    has_xn, has_xp = number(sx < nstream - 1), number(sx > 0)
+    has_yn, has_yp = number(sy < nspan - 1), number(sy > 0)
+
+    column = lax.rem(lane, 4)
+    far_left, near_left = column >= 2, column == 2
+    gate2 = jnp.where(far_left, has_xp, has_xn)
+    sign2 = jnp.where(far_left, -C2 * has_xp, C2 * has_xn)
+    near_right = column == 1
+    gate1 = jnp.where(near_left, 4.0 * has_xp, jnp.where(near_right, 4.0 * has_xn, 0.0))
+    sign1 = jnp.where(near_left, C1 * has_xp, jnp.where(near_right, -C1 * has_xn, 0.0))
+
+    def columns(i):
         return (
-            pltpu.roll(jnp.where(index < 1, h, t), size - 1, axis),
-            pltpu.roll(jnp.where(index < 2, h, t), size - 2, axis),
-            pltpu.roll(jnp.where(index >= size - 1, h, t), 1, axis),
-            pltpu.roll(jnp.where(index >= size - 2, h, t), 2, axis),
-        )
-
-    C1, C2 = 2.0 / 3.0, 1.0 / 12.0
+            jnp.where(far_left, pltpu.roll(xh_l[i], 2, 1), pltpu.roll(xh_r[i], 126, 1)),
+            jnp.where(near_left, pltpu.roll(xh_l[i], 1, 1), pltpu.roll(xh_r[i], 127, 1)),
+        )
+
+    a2, a1 = columns(NV)
+    w2 = sign2 * a2 - gate2 * xpack[NV + 1]
+    w1 = sign1 * a1 + gate1 * xpack[NV + 1]
+    for v in range(NV):
+        s2, s1 = columns(v)
+        xcor[v] = w2 * s2 + w1 * s1
+    edge = jnp.logical_or(lane < 2, lane >= 126)
+
+    ygate2 = jnp.where(row < 2, has_yp, jnp.where(row >= 6, has_yn, 0.0))
+    ysign2 = jnp.where(row < 2, -C2 * has_yp, jnp.where(row >= 6, C2 * has_yn, 0.0))
+    ygate1 = jnp.where(row < 1, 4.0 * has_yp, jnp.where(row >= 7, 4.0 * has_yn, 0.0))
+    ysign1 = jnp.where(row < 1, C1 * has_yp, jnp.where(row >= 7, -C1 * has_yn, 0.0))
+    first = row < 1
+
+    def nearest(h):
+        return jnp.where(first, pltpu.roll(h, 7, 0), pltpu.roll(h, 1, 0))
 
     def level(k, carry):
         d = dmp[k]
-        d4 = 4.0 * d
+        a2 = yh[NV, k]
+        w2 = ysign2 * a2 - ygate2 * d
+        w1 = ysign1 * nearest(a2) + ygate1 * d
         shift = 126 - 4 * k
-        hx = [pltpu.roll(xh_l[i], shift, 1) for i in range(NV + 1)]
-        xp1, xp2, xm1, xm2 = around(spx[k], hx[NV], lane, 128, 1)
-        yp1, yp2, ym1, ym2 = around(spy[k], yh[NV, k], row, 8, 0)
-        zm2, zm1, zp1, zp2 = spz[k], spz[k + 1], spz[k + 3], spz[k + 4]
-        wx = ((d4 - C1 * xp1) * gx_p1, (C2 * xp2 - d) * gx_p2, (d4 + C1 * xm1) * gx_m1, (-d - C2 * xm2) * gx_m2)
-        wy = ((d4 - C1 * yp1) * gy_p1, (C2 * yp2 - d) * gy_p2, (d4 + C1 * ym1) * gy_m1, (-d - C2 * ym2) * gy_m2)
-        wz = (d4 - C1 * zp1, C2 * zp2 - d, d4 + C1 * zm1, -d - C2 * zm2)
-        wc = -18.0 * d
         rhs = []
         for v in range(NV):
-            t = st[v, k + 2]
-            acc = src[v, k] + wc * t
-            zs = (st[v, k + 3], st[v, k + 4], st[v, k + 1], st[v, k])
-            accz = wz[0] * zs[0] + wz[1] * zs[1] + wz[2] * zs[2] + wz[3] * zs[3]
-            xs = around(t, hx[v], lane, 128, 1)
-            accx = wx[0] * xs[0] + wx[1] * xs[1] + wx[2] * xs[2] + wx[3] * xs[3]
-            ys = around(t, yh[v, k], row, 8, 0)
-            accy = wy[0] * ys[0] + wy[1] * ys[1] + wy[2] * ys[2] + wy[3] * ys[3]
-            rhs.append((acc + accz) + (accx + accy))
+            h = yh[v, k]
+            cor = jnp.where(edge, pltpu.roll(xcor[v], shift, 1), 0.0)
+            rhs.append((src[v, k] + cor) + (w2 * h + w1 * nearest(h)))
         new = []
         for c in range(NV):
             f = left[c, 0] * rhs[0]
@@ -341,7 +407,7 @@
             (v_s[c, k] + far_s[c, k] * carry[c][1] - near_s[c, k] * carry[c][0], carry[c][0]) for c in range(NV)
         )
 
-    firsts = lax.fori_loop(0, K - 2, back, tuple((zero, zero) for _ in range(NV)))
+    firsts = loop(0, K - 2, back, tuple((zero, zero) for _ in range(NV)), 5)
     for c in range(NV):
         w0, w1 = firsts[c]
         v1 = ends[c][0]
@@ -363,7 +429,7 @@
             tri[j, i] = val
         return t
 
-    lax.fori_loop(0, nnorm, block_factor, (zero, zero, zero, zero))
+    loop(0, nnorm, block_factor, (zero, zero, zero, zero), 4)
 
     recv_all(rr_send, rr, r_send, r_recv)
 
@@ -376,7 +442,7 @@
         rr[j, 1] = n1
         return (n0, n1)
 
-    lax.fori_loop(0, nnorm, block_forward, (zero, zero))
+    loop(0, nnorm, block_forward, (zero, zero), 4)
 
     def block_back(i, carry):
         j = nnorm - 1 - i
@@ -387,25 +453,25 @@
         sp[j + 1, 1] = n1
         return (n0, n1)
 
-    lax.fori_loop(0, nnorm, block_back, (zero, zero))
+    loop(0, nnorm, block_back, (zero, zero), 4)
     sp[0, 0] = zero
     sp[0, 1] = zero
 
     def home(t, first, count):
         return remote(
-            sp.at[pl.ds(t, 2), :, 0:count, :], xsep.at[:, :, first:first + count, lax.rem(sz, 8), :],
+            sp.at[pl.ds(t, 2), :, 0:count, :], xsep.at[:, :, first:first + count, line(sz), :],
             s_send.at[t], s_recv.at[sz], (sx, sy, t),
         )
 
     def home_in(t, first, count):
         return remote(
-            sp.at[0:2, :, 0:count, :], xsep.at[:, :, first:first + count, lax.rem(t, 8), :],
+            sp.at[0:2, :, 0:count, :], xsep.at[:, :, first:first + count, line(t), :],
             s_send.at[t], s_recv.at[t], (sx, sy, t),
         )
 
     def home_own(first, count):
         return pltpu.make_async_copy(
-            sp.at[pl.ds(sz, 2), :, 0:count, :], xsep.at[:, :, first:first + count, lax.rem(sz, 8), :], s_recv.at[sz]
+            sp.at[pl.ds(sz, 2), :, 0:count, :], xsep.at[:, :, first:first + count, line(sz), :], s_recv.at[sz]
         )
 
     def home_all(first, count):
@@ -447,7 +513,7 @@
         emit(k, [n[0] for n in new])
         return tuple(new)
 
-    lax.fori_loop(0, K - 2, final, tuple(own_s))
+    loop(0, K - 2, final, tuple(own_s), 1)
 
     for c in halos:
         c.wait_send()
@@ -483,7 +549,7 @@
             out_specs=pl.BlockSpec(memory_space=pltpu.VMEM),
             scratch_shapes=[
                 vm(NV, K + 4), vm(K + 4), vm(K), vm(K), vm(K), vm(NV, K), vm(K), vm(K),
-                vm(NV + 1, K), vm(NV + 1), vm(NV + 1), vm(NV + 1),
+                vm(NV + 1, K), vm(NV + 1, 2), vm(NV + 1, 2), vm(NV + 2), vm(NV + 1), vm(NV + 1), vm(NV),
                 per(), per(), per(), per(), per(), per(), per(),
                 vm(4, NV), vm(4, NV), vm(4, NV), vm(4, NV), vm(4, NV), vm(8, NV), vm(8, NV), vm(nnorm + 1, 8),
                 vm(4, NV), vm(nnorm + 1, 4), vm(nnorm, 12), vm(nnorm + 1, 2), vm(2, 2, NV), vm(2),

time: 45.7 us -> 42.7 us (0.934)
  Pallas kernels: 44.5 us -> 41.7 us
    pallas_call x1, Pallas kernels: 44.5 us -> 41.7 us  [step(): pl.pallas_call(functools.partial(kernel, nstream, nspan, nnorm), out_shap...]
where the time goes in v3:
time: 42.7 us; the launch traced here: 42.5 us
  Pallas kernels  41.7 us (98%)
  local copies, waits for them, and re-layouts  0.84 us (2%)
    pallas_call x1, Pallas kernels, step(): pl.pallas_call(functools.partial(kernel, nstream, nspan, nnorm), out_shap...  41.7 us

profile of v3, /device:TPU:24, one launch (start us, length us, event | category | flops | bytes accessed | tf_op | source)
XLA Modules:
  0.0 42.5 jit_solution(12840201917787340950)
XLA Ops:
  0.0 41.7 %shard_map.91 = f32[5,32,8,128]{3,2,1,0:T(8,128)S(1)} custom-call(f32[5,32,8,128]{3,2,1,0:T(8,128)} %state.1, f32[3,32,8,128]{3,2,1,0:T(8,128)} %speeds.1, f32[32,8,128]{2,1,0:T(8,128)} %damping.1, f32[5,32,8,128]{3,2,1,0:T(8,128)} %source.1, f32[32,8,128]{2,1,0:T(8,128)} %nstiff.1, f32[32,8,128]{2,1,0:T(8,128)} %wstiff.1, f32[5]{0:T(128)} %rates_in.1, ...), custom_call_target="tpu_custom_call" | custom-call | flops 20000000 | bytes 2900000 | tf_op jit(solution)/shard_map/pallas_call | solution.py:545
  41.7 0.8 %copy.11 = f32[5,32,8,128]{3,2,1,0:T(8,128)} copy(f32[5,32,8,128]{3,2,1,0:T(8,128)S(1)} %shard_map.91) | data formatting | bytes 1310720

commit v4 on v3

--- a/solution.py
+++ b/solution.py
@@ -249,8 +249,58 @@
             p[2] * q[0] + p[3] * q[2], p[2] * q[1] + p[3] * q[3],
         )
 
-    for c in range(NV):
-        four = lambda ref, c=c: tuple(ref[e, c] for e in range(4))
+    def heavy(t):
+        return lax.rem(t, 2) == 0
+
+    def line(t):
+        return t // 2
+
+    def either(t, do):
+        pl.when(heavy(t))(lambda: do(0, 3))
+        pl.when(jnp.logical_not(heavy(t)))(lambda: do(3, 2))
+
+    def scatter(rows, land, s, r, t, first, count):
+        return remote(
+            rows.at[:, first:first + count, line(t), :], land.at[sz, :, 0:count, :],
+            s.at[t], r.at[sz], (sx, sy, t),
+        )
+
+    def scatter_in(rows, land, s, r, t, first, count):
+        return remote(
+            rows.at[:, first:first + count, 0, :], land.at[t, :, 0:count, :], s.at[t], r.at[t], (sx, sy, t)
+        )
+
+    def scatter_own(rows, land, r, first, count):
+        return pltpu.make_async_copy(
+            rows.at[:, first:first + count, line(sz), :], land.at[sz, :, 0:count, :], r.at[sz]
+        )
+
+    def send_all(rows, land, s, r):
+        @pl.loop(0, nnorm - 1)
+        def _(i):
+            t = peer(i)
+            either(t, lambda first, count: scatter(rows, land, s, r, t, first, count).start())
+
+        either(sz, lambda first, count: scatter_own(rows, land, r, first, count).start())
+
+    def recv_all(rows, land, s, r):
+        def every(first, count):
+            @pl.loop(1, nnorm)
+            def _(d):
+                scatter_in(rows, land, s, r, lax.rem(sz + d, nnorm), first, count).wait_recv()
+
+            scatter_own(rows, land, r, first, count).wait()
+
+        either(sz, every)
+
+    def drain_all(rows, land, s, r):
+        @pl.loop(1, nnorm)
+        def _(d):
+            t = lax.rem(sz + d, nnorm)
+            either(t, lambda first, count: scatter(rows, land, s, r, t, first, count).wait_send())
+
+    def blocks(c):
+        four = lambda ref: tuple(ref[e, c] for e in range(4))
         n30, a30, a31, b30, b31 = near_s[c, K - 2], a_s[c, K - 2], a_s[c, K - 1], b_s[c, K - 2], b_s[c, K - 1]
         d = inverse(four(n_send), four(a_recv))
         p = times(d, (a30 - n30 * a31, b30 - n30 * b31, a31, b31))
@@ -263,57 +313,19 @@
             pq[i, c] = p[i]
             pq[4 + i, c] = q[i]
 
-    def heavy(t):
-        return lax.rem(t, 2) == 0
-
-    def line(t):
-        return t // 2
-
-    def either(t, do):
-        pl.when(heavy(t))(lambda: do(0, 3))
-        pl.when(jnp.logical_not(heavy(t)))(lambda: do(3, 2))
-
-    def scatter(rows, land, s, r, t, first, count):
-        return remote(
-            rows.at[:, first:first + count, line(t), :], land.at[sz, :, 0:count, :],
-            s.at[t], r.at[sz], (sx, sy, t),
-        )
-
-    def scatter_in(rows, land, s, r, t, first, count):
-        return remote(
-            rows.at[:, first:first + count, 0, :], land.at[t, :, 0:count, :], s.at[t], r.at[t], (sx, sy, t)
-        )
-
-    def scatter_own(rows, land, r, first, count):
-        return pltpu.make_async_copy(
-            rows.at[:, first:first + count, line(sz), :], land.at[sz, :, 0:count, :], r.at[sz]
-        )
-
-    def send_all(rows, land, s, r):
+    for first, count in ((3, 2), (0, 3)):
+        for c in range(first, first + count):
+            blocks(c)
+
         @pl.loop(0, nnorm - 1)
         def _(i):
             t = peer(i)
-            either(t, lambda first, count: scatter(rows, land, s, r, t, first, count).start())
-
-        either(sz, lambda first, count: scatter_own(rows, land, r, first, count).start())
-
-    def recv_all(rows, land, s, r):
-        def every(first, count):
-            @pl.loop(1, nnorm)
-            def _(d):
-                scatter_in(rows, land, s, r, lax.rem(sz + d, nnorm), first, count).wait_recv()
-
-            scatter_own(rows, land, r, first, count).wait()
-
-        either(sz, every)
-
-    def drain_all(rows, land, s, r):
-        @pl.loop(1, nnorm)
-        def _(d):
-            t = lax.rem(sz + d, nnorm)
-            either(t, lambda first, count: scatter(rows, land, s, r, t, first, count).wait_send())
-
-    send_all(pq, rc, c_send, c_recv)
+
+            @pl.when(heavy(t) if count == 3 else jnp.logical_not(heavy(t)))
+            def _():
+                scatter(pq, rc, c_send, c_recv, t, first, count).start()
+
+    either(sz, lambda first, count: scatter_own(pq, rc, c_recv, first, count).start())
 
     lax.fori_loop(K // 4, K, interior, 0)
 

time: 42.7 us -> 43.2 us (1.012)
  Pallas kernels: 41.7 us -> 42.2 us
    pallas_call x1, Pallas kernels: 41.7 us -> 42.2 us  [step(): pl.pallas_call(functools.partial(kernel, nstream, nspan, nnorm), out_shap...]
where the time goes in v4:
time: 43.2 us; the launch traced here: 43.1 us
  Pallas kernels  42.2 us (98%)
  local copies, waits for them, and re-layouts  0.84 us (2%)
    pallas_call x1, Pallas kernels, step(): pl.pallas_call(functools.partial(kernel, nstream, nspan, nnorm), out_shap...  42.2 us

profile of v4, /device:TPU:24, one launch (start us, length us, event | category | flops | bytes accessed | tf_op | source)
XLA Modules:
  0.0 43.1 jit_solution(2038222318169381900)
XLA Ops:
  0.0 42.2 %shard_map.91 = f32[5,32,8,128]{3,2,1,0:T(8,128)S(1)} custom-call(f32[5,32,8,128]{3,2,1,0:T(8,128)} %state.1, f32[3,32,8,128]{3,2,1,0:T(8,128)} %speeds.1, f32[32,8,128]{2,1,0:T(8,128)} %damping.1, f32[5,32,8,128]{3,2,1,0:T(8,128)} %source.1, f32[32,8,128]{2,1,0:T(8,128)} %nstiff.1, f32[32,8,128]{2,1,0:T(8,128)} %wstiff.1, f32[5]{0:T(128)} %rates_in.1, ...), custom_call_target="tpu_custom_call" | custom-call | flops 20000000 | bytes 2900000 | tf_op jit(solution)/shard_map/pallas_call | solution.py:557
  42.2 0.8 %copy.11 = f32[5,32,8,128]{3,2,1,0:T(8,128)} copy(f32[5,32,8,128]{3,2,1,0:T(8,128)S(1)} %shard_map.91) | data formatting | bytes 1310720
